TPU v7x, 32 devices: a whole 2x2x4 slice. The times are simulated.
32 devices in a mesh: row: 4 (over x, core), col: 8 (over z, y).
Axes of the slice: x: 2, y: 2, z: 4, core: 2. Of those that a mesh axis runs over, the one named last changes fastest.
Arguments:
- features: bfloat16 [8192, 512], P(('col', 'row')), may hold values from -6 to 6
- weight: bfloat16 [512, 512], replicated, may hold values from -0.25 to 0.25
- entry_values: bfloat16 [4, 8, 32, 128, 128], P('row', 'col'), may hold values from 0.0009994507 to 0.019897461
- block_rows: int32 [4, 8, 32], P('row', 'col'), may hold values from 0 to 15
- block_cols: int32 [4, 8, 32], P('row', 'col'), may hold values from 0 to 7
- entry_counts: int32 [4, 8], P('row', 'col'), may hold values from 8 to 32, as said below
- cotangent: bfloat16 [8192, 512], P(('row', 'col')), may hold values from -1.5 to 1.5
Outputs:
- output: bfloat16 [8192, 512], P(('row', 'col'))
- grad_features: bfloat16 [8192, 512], P(('col', 'row'))
- grad_weight: float32 [512, 512], replicated
Inputs may be any that keep to these rules, and one draw needn't show every extreme that they name: `entry_counts`: each grid cell has at least 8 live slots; at least one cell has all 32 live.
All inputs are finite; a program needn't handle non-finite values.
Results may differ from a plain program's by a relative error of at most 0.022.
Values may be sent and summed in bfloat16 or wider, within the bound.
A program may use at most 128 MiB of HBM per device.

v0:
```python
import jax
import jax.numpy as jnp
from jax import lax
from jax.sharding import PartitionSpec as P


def block_terms(values, source_ids, target_ids, live_count, source, target_blocks, transpose):
    entry_total = values.shape[0]
    block_side = values.shape[1]
    feature_count = source.shape[1]
    group_size = min(32, entry_total)
    source_tiles = source.reshape(-1, block_side, feature_count)

    def one_group(group_index, running):
        first_entry = group_index * group_size
        tiles = jnp.take(source_tiles, source_ids, axis=0)
        if transpose:
            products = jnp.einsum("kba,kbf->kaf", values, tiles, preferred_element_type=jnp.float32)
        else:
            products = jnp.einsum("kab,kbf->kaf", values, tiles, preferred_element_type=jnp.float32)
        alive_mask = (first_entry + jnp.arange(group_size) < live_count).astype(jnp.float32)
        return running.at[target_ids].add(products * alive_mask[:, None, None])

    zero_sum = jnp.zeros((target_blocks, block_side, feature_count), jnp.float32)
    trip_count = entry_total // group_size
    running = lax.fori_loop(0, trip_count, one_group, zero_sum)
    return running.reshape(target_blocks * block_side, feature_count)


def silu_slope(summed):
    sigmoid_value = jax.nn.sigmoid(summed)
    return sigmoid_value * (1.0 + summed * (1.0 - sigmoid_value))


def shards(features, weight, entry_values, block_rows, block_cols, entry_counts, cotangent):
    values = entry_values[0, 0]
    row_ids = block_rows[0, 0]
    col_ids = block_cols[0, 0]
    live_count = entry_counts[0, 0]
    local_rows = features.shape[0]
    block_side = values.shape[1]
    row_span = lax.axis_size("col") * local_rows
    col_span = lax.axis_size("row") * local_rows
    projected = jnp.dot(features, weight, preferred_element_type=jnp.float32).astype(jnp.bfloat16)
    panel = lax.all_gather(projected, "row", axis=0, tiled=True)
    forward_terms = block_terms(
        values, col_ids, row_ids, live_count, panel, row_span // block_side, False
    )
    summed = lax.psum(forward_terms.astype(jnp.bfloat16), "col").astype(jnp.float32)
    position = lax.axis_index("col") * local_rows
    own_sum = lax.dynamic_slice_in_dim(summed, position, local_rows, 0)
    output = jax.nn.silu(own_sum).astype(jnp.bfloat16)
    incoming = lax.all_gather(cotangent, "col", axis=0, tiled=True)
    upstream = (incoming.astype(jnp.float32) * silu_slope(summed)).astype(jnp.bfloat16)
    backward_terms = block_terms(
        values, row_ids, col_ids, live_count, upstream, col_span // block_side, True
    )
    grad_projected = lax.psum_scatter(
        backward_terms.astype(jnp.bfloat16), "row", scatter_dimension=0, tiled=True
    )
    weight_term = lax.dot_general(
        features, grad_projected, (((0,), (0,)), ((), ())), preferred_element_type=jnp.float32
    )
    grad_weight = lax.psum(weight_term, ("row", "col"))
    grad_features = lax.dot_general(
        grad_projected, weight, (((1,), (1,)), ((), ())), preferred_element_type=jnp.float32
    ).astype(jnp.bfloat16)
    return (output, grad_features, grad_weight)


def solution(mesh):
    placed = (
        P(("col", "row"), None),
        P(),
        P("row", "col", None, None, None),
        P("row", "col", None),
        P("row", "col", None),
        P("row", "col"),
        P(("row", "col"), None),
    )
    return jax.shard_map(
        shards,
        mesh=mesh,
        in_specs=placed,
        out_specs=(P(("row", "col"), None), P(("col", "row"), None), P()),
        check_vma=False,
    )
```

profile of v0, /device:TPU:0, one launch (start us, length us, event | category | flops | bytes accessed | tf_op | source)
XLA Modules:
  0.0 432.9 jit_solution(9976734969442285223)
XLA Ops:
  7.2 0.0 copy-start
  7.2 0.0 all-gather.3.cloned.1.call-start
  7.2 2.2 convolution_convert_fusion.1
  9.4 0.0 all-gather.3.cloned.1.call-update
  9.5 0.0 all-reduce.3.cloned.1.call-start
  10.2 0.7 fusion.15
  10.8 0.7 fusion.14
  11.5 0.7 compare_convert_fusion
  12.1 17.5 %all-gather.3.cloned.1.call-done = bf16[1024,512]{1,0:T(8,128)(2,1)} async-done(((bf16[256,512]{1,0:T(8,128)(2,1)}), bf16[1024,512]{1,0:T(8,128)(2,1)}) %all-gather.3.cloned.1.call-update) | async-done | bytes 1048592 | tf_op jit(solution)/shard_map/all_gather | solution.py:45
  29.6 4.0 gather_fusion
  33.6 0.0 copy-done
  33.6 7.1 %multiply_bitcast_fusion.1 = f32[32,128,512]{1,2,0:T(8,128)} fusion(f32[32]{0:T(128)S(1)} %get-tuple-element.49, bf16[32,128,512]{2,1,0:T(8,128)(2,1)} %gather_fusion, pred[32]{0:T(512)(128)(4,1)S(1)} %get-tuple-element.50, bf16[1,1,32,128,128]{4,3,2,1,0:T(8,128)(2,1)S(1)} %copy-done), kind=kOutput, calls=%fused_computation.5 | convolution fusion | flops 541065216 | bytes 13631648 | tf_op jit(solution)/shard_map/while/body/eval_jaxpr/kab,kbf->kaf/dot_general | solution.py:20
  40.7 9.0 %copy.14 = f32[32,128,512]{2,1,0:T(8,128)} copy(f32[32,128,512]{1,2,0:T(8,128)} %multiply_bitcast_fusion.1) | data formatting | bytes 16777216 | tf_op jit(solution)/shard_map/while/body/eval_jaxpr/mul | solution.py:22
  49.7 2.5 broadcast_in_dim.38
  52.2 18.2 %scatter_fusion = f32[16,128,512]{2,1,0:T(8,128)} fusion(f32[16,128,512]{2,1,0:T(8,128)} %broadcast_in_dim.38, s32[32]{0:T(128)S(1)} %fusion.14, f32[32,128,512]{2,1,0:T(8,128)} %copy.14), kind=kCustom, calls=%fused_computation.2 | custom fusion | flops 2097152 | bytes 25165952 | tf_op jit(solution)/shard_map/while/body/eval_jaxpr/scatter-add | solution.py:22
  70.4 0.0 copy-start.5
  70.4 3.8 convert_element_type.42
  74.2 0.0 all-reduce.3.cloned.1.call-update
  74.3 0.0 all-gather.5.cloned.1.call-start
  74.3 0.7 all-gather.5.cloned.1.call-update
  75.0 0.0 reduce-scatter.2.cloned.1.call-start
  75.1 0.0 copy-done.5
  75.1 101.6 %all-reduce.3.cloned.1.call-done = bf16[2048,512]{1,0:T(8,128)(2,1)} async-done(((bf16[2048,512]{1,0:T(8,128)(2,1)}), bf16[2048,512]{1,0:T(8,128)(2,1)}) %all-reduce.3.cloned.1.call-update) | async-done | bytes 2097168 | tf_op jit(solution)/shard_map/psum | solution.py:49
  176.7 51.2 %all-gather.5.cloned.1.call-done = bf16[2048,512]{1,0:T(8,128)(2,1)} async-done(((bf16[256,512]{1,0:T(8,128)(2,1)}), bf16[2048,512]{1,0:T(8,128)(2,1)}) %all-gather.5.cloned.1.call-update) | async-done | bytes 2097168 | tf_op jit(solution)/shard_map/all_gather | solution.py:53
  227.9 3.9 multiply_convert_fusion
  231.8 2.8 gather_fusion.1
  234.6 7.2 %multiply_bitcast_fusion = f32[32,128,512]{1,2,0:T(8,128)} fusion(f32[32]{0:T(128)S(1)} %get-tuple-element.49, bf16[32,128,512]{2,1,0:T(8,128)(2,1)} %gather_fusion.1, pred[32]{0:T(512)(128)(4,1)S(1)} %compare_and_fusion, bf16[1,1,32,128,128]{4,3,2,1,0:T(8,128)(2,1)S(1)} %copy-done), kind=kOutput, calls=%fused_computation.4 | convolution fusion | flops 541065216 | bytes 13631648 | tf_op jit(solution)/shard_map/while/body/eval_jaxpr/kba,kbf->kaf/dot_general | solution.py:18
  241.8 9.0 %copy.16 = f32[32,128,512]{2,1,0:T(8,128)} copy(f32[32,128,512]{1,2,0:T(8,128)} %multiply_bitcast_fusion) | data formatting | bytes 16777216 | tf_op jit(solution)/shard_map/while/body/eval_jaxpr/mul | solution.py:22
  250.8 0.2 broadcast_in_dim.41
  251.0 11.8 %scatter_fusion.1 = f32[8,128,512]{2,1,0:T(8,128)S(1)} fusion(f32[8,128,512]{2,1,0:T(8,128)S(1)} %broadcast_in_dim.41, s32[32]{0:T(128)S(1)} %fusion.15, f32[32,128,512]{2,1,0:T(8,128)} %copy.16), kind=kCustom, calls=%fused_computation.3 | custom fusion | flops 2097152 | bytes 25165952 | tf_op jit(solution)/shard_map/while/body/eval_jaxpr/scatter-add | solution.py:22
  262.8 0.0 copy-start.3
  262.8 1.1 convert_element_type.48
  263.9 0.0 copy-start.1
  263.9 0.0 reduce-scatter.2.cloned.1.call-update
  263.9 0.0 all-reduce.5.cloned.1.call-start
  264.0 23.5 %reduce-scatter.2.cloned.1.call-done = bf16[256,512]{1,0:T(8,128)(2,1)} async-done(((bf16[1024,512]{1,0:T(8,128)(2,1)}), bf16[256,512]{1,0:T(8,128)(2,1)}) %reduce-scatter.2.cloned.1.call-update) | async-done | bytes 262160 | tf_op jit(solution)/shard_map/reduce_scatter | solution.py:58
  287.5 0.0 copy-done.3
  287.5 2.2 convolution_bitcast_fusion
  289.8 0.0 all-reduce.5.cloned.1.call-update
  289.8 0.0 copy-done.1
  289.8 0.0 copy-start.2
  289.8 0.6 convert_element_type.44
  290.4 0.9 multiply_convert_fusion.1
  291.3 0.0 copy-done.4
  291.3 0.0 copy-done.2
  291.3 1.0 convolution_convert_fusion
  292.3 131.5 %all-reduce.5.cloned.1.call-done = f32[512,512]{0,1:T(8,128)} async-done(((f32[512,512]{0,1:T(8,128)}), f32[512,512]{0,1:T(8,128)}) %all-reduce.5.cloned.1.call-update) | async-done | bytes 1048592 | tf_op jit(solution)/shard_map/psum | solution.py:64
  423.8 2.5 copy.17
  (4 shorter events, 0.0 us)
Async XLA Ops:
  7.2 26.4 %copy-start = (bf16[1,1,32,128,128]{4,3,2,1,0:T(8,128)(2,1)S(1)}, bf16[1,1,32,128,128]{4,3,2,1,0:T(8,128)(2,1)}, u32[]{:S(2)}) copy-start(bf16[1,1,32,128,128]{4,3,2,1,0:T(8,128)(2,1)} %param.9) | copy-start | bytes 3145732
  7.2 22.4 %all-gather.3.cloned.1.call-start = ((), (), s32[]{:S(2)}) async-start(), calls=%async_computation.1 | async-start | bytes 1310720 | tf_op jit(solution)/shard_map/all_gather | solution.py:45
  9.5 167.2 %all-reduce.3.cloned.1.call-start = ((), (), s32[]{:S(2)}) async-start(), calls=%async_computation.2 | async-start | bytes 4194304 | tf_op jit(solution)/shard_map/psum | solution.py:49
  70.4 4.6 %copy-start.5 = (s32[1,1,32]{2,1,0:T(1,128)S(1)}, s32[1,1,32]{2,1,0:T(1,128)}, u32[]{:S(2)}) copy-start(s32[1,1,32]{2,1,0:T(1,128)} %param.10) | copy-start | bytes 388
  74.3 153.6 %all-gather.5.cloned.1.call-start = ((), (), s32[]{:S(2)}) async-start(), calls=%async_computation.3 | async-start | bytes 2359296 | tf_op jit(solution)/shard_map/all_gather | solution.py:53
  75.0 212.5 %reduce-scatter.2.cloned.1.call-start = ((), (), s32[]{:S(2)}) async-start(), calls=%async_computation.4 | async-start | bytes 1310720 | tf_op jit(solution)/shard_map/reduce_scatter | solution.py:58
  262.8 24.7 %copy-start.3 = (bf16[256,512]{1,0:T(8,128)(2,1)S(1)}, bf16[256,512]{1,0:T(8,128)(2,1)}, u32[]{:S(2)}) copy-start(bf16[256,512]{1,0:T(8,128)(2,1)} %param.7) | copy-start | bytes 786436
  263.9 25.9 %copy-start.1 = (bf16[2048,512]{1,0:T(8,128)(2,1)S(1)}, bf16[2048,512]{1,0:T(8,128)(2,1)}, u32[]{:S(2)}) copy-start(bf16[2048,512]{1,0:T(8,128)(2,1)} %all-reduce.3.cloned.1.call-done) | copy-start | bytes 6291460
  263.9 159.9 %all-reduce.5.cloned.1.call-start = ((), (), s32[]{:S(2)}) async-start(), calls=%async_computation.5 | async-start | bytes 2097152 | tf_op jit(solution)/shard_map/psum | solution.py:64
  289.8 1.5 copy-start.4
  289.8 1.5 copy-start.2
Sparse Core Ops, SparseCore 0:
  10.1 19.4 all-gather.2
  74.4 102.2 all-reduce.2
  178.8 49.0 all-gather.4
  264.0 23.4 reduce-scatter.1
  293.9 129.8 all-reduce.4
where the time goes:
time: 434 us; the launch traced here: 433 us
  waiting for transfers between devices  326 us (75%)
  other arithmetic  42.2 us (10%)
  local copies, waits for them, and re-layouts  30.1 us (7%)
  matrix products  19.8 us (5%)
  between operations  14.5 us (3%)
    psum x1, waiting for transfers between devices, shards(): grad_weight = lax.psum(weight_term, ('row', 'col'))  131 us
    psum x1, waiting for transfers between devices, shards(): lax.psum(forward_terms.astype(jnp.bfloat16), 'col').astype(jnp.float32)  102 us
    all_gather x1, waiting for transfers between devices, shards(): incoming = lax.all_gather(cotangent, 'col', axis=0, tiled=True)  51.2 us
    scatter-add x2, other arithmetic, one_group(): return running.at[target_ids].add(products * alive_mask[:, None, None])  29.9 us
    reduce_scatter x1, waiting for transfers between devices, shards(): lax.psum_scatter(backward_terms.astype(jnp.bfloat16), 'row', scatter_dime...  23.5 us
    mul x2, local copies, waits for them, and re-layouts, one_group(): return running.at[target_ids].add(products * alive_mask[:, None, None])  18 us
    all_gather x1, waiting for transfers between devices, shards(): panel = lax.all_gather(projected, 'row', axis=0, tiled=True)  17.5 us
  transfers between devices with their start and end apart: 5, of which 5 were waited for; matrix products, arithmetic and copies ran while one was open for 1% of the time, Pallas kernels for 0%

commit v1 on v0

v1 whole, which is shorter than its diff:
```python
import functools

import jax
import jax.numpy as jnp
from jax import lax
from jax.experimental import pallas as pl
from jax.experimental.pallas import tpu as pltpu
from jax.sharding import PartitionSpec as P

MESH = pl.DeviceIdType.MESH
BF = jnp.bfloat16
F32 = jnp.float32
VMEM_LIMIT = 60 * 1024 * 1024


def densify(values, rows, cols, count, dense):
    side = values.shape[1]
    per = dense.shape[1] // side

    def clear(j, carry):
        dense[j] = jnp.zeros(dense.shape[1:], dense.dtype)
        return carry

    lax.fori_loop(0, dense.shape[0], clear, 0)

    def add(k, carry):
        r, c = rows[k], cols[k]
        spot = (
            r // per,
            pl.ds(pl.multiple_of((r % per) * side, side), side),
            pl.ds(pl.multiple_of(c * side, side), side),
        )
        dense[spot] = (dense[spot].astype(F32) + values[k].astype(F32)).astype(dense.dtype)
        return carry

    lax.fori_loop(0, count[0], add, 0)


def dot(a, b, dims):
    return lax.dot_general(a, b, (dims, ((), ())), preferred_element_type=F32)


NN = ((1,), (0,))
TN = ((0,), (0,))
NT = ((1,), (1,))


def layer(n_row, n_col, feat, weight, dense, cot, out, gfeat, gweight, s):
    ri_n = 2
    ro_n = n_row // ri_n
    co_n = 4
    ci_n = n_col // co_n
    rows, width = feat.shape
    r, c = lax.axis_index("row"), lax.axis_index("col")
    ro, ri = r // ri_n, r % ri_n
    co, ci = c // ci_n, c % ci_n
    span = n_row * rows

    def send(src, dst, ss, rs, row, col):
        return pltpu.make_async_remote_copy(
            src_ref=src, dst_ref=dst, send_sem=ss, recv_sem=rs, device_id=(row, col), device_id_type=MESH
        )

    def arrived(dst, rs, ss):
        send(dst, dst, ss, rs, r, lax.rem(c + 1, n_col)).wait_recv()

    barrier = pltpu.get_barrier_semaphore()
    for d in range(1, n_row):
        pl.semaphore_signal(barrier, inc=1, device_id=(lax.rem(r + d, n_row), c), device_id_type=MESH)
    for d in range(1, n_col):
        pl.semaphore_signal(barrier, inc=1, device_id=(r, lax.rem(c + d, n_col)), device_id_type=MESH)
    pl.semaphore_wait(barrier, n_row + n_col - 2)

    mate = ro * ri_n + (1 - ri)
    pending = []
    for d in range(1, ro_n):
        peer = lax.rem(ro + d, ro_n) * ri_n + ri
        cp = send(feat, s["panel"].at[r], s["pss"].at[d - 1], s["prs"].at[r], peer, c)
        cp.start()
        pending.append(cp)
    cp = send(feat, s["panel"].at[r], s["pss"].at[ro_n - 1], s["prs"].at[r], mate, c)
    cp.start()
    pending.append(cp)
    s["panel"][r] = feat[...]

    def project(slot):
        s["proj"][slot] = dot(s["panel"][slot], weight[...], NN).astype(BF)

    project(r)
    for d in range(1, ro_n):
        slot = lax.rem(ro - d + ro_n, ro_n) * ri_n + ri
        arrived(s["panel"].at[slot], s["prs"].at[slot], s["pss"].at[0])
        cp = send(s["panel"].at[slot], s["panel"].at[slot], s["pss"].at[ro_n - 1 + d], s["prs"].at[slot], mate, c)
        cp.start()
        pending.append(cp)
        project(slot)
    for d in range(ro_n):
        slot = lax.rem(ro - d + ro_n, ro_n) * ri_n + (1 - ri)
        arrived(s["panel"].at[slot], s["prs"].at[slot], s["pss"].at[0])
        project(slot)

    def far(k):
        table = ((3, 2, 1, 0), (3, 0, 2, 1), (0, 3, 1, 2), (0, 1, 2, 3))

        def entry(pos):
            picked = jnp.int32(table[pos][co_n - 1])
            for q in range(co_n - 1):
                picked = jnp.where(k == q, table[pos][q], picked)
            return picked

        picked = entry(co_n - 1)
        for pos in range(co_n - 1):
            picked = jnp.where(co == pos, entry(pos), picked)
        return picked

    def fetch(j, slot):
        return pltpu.make_async_copy(dense.at[j], s["tile"].at[slot], s["ts"].at[slot])

    fetch(far(0) * ci_n + lax.rem(ci + 1, ci_n), 0).start()

    def forward(k, carry):
        t = far(k)
        for d in list(range(1, ci_n)) + [0]:
            step = k * ci_n + (d - 1 if d else ci_n - 1)
            slot = step % 2
            target = lax.rem(ci + d, ci_n)
            j = t * ci_n + target
            ahead = step + 1
            if d:
                after = t * ci_n + lax.rem(ci + (d + 1) % ci_n, ci_n)
                fetch(after, ahead % 2).start()
            else:
                @pl.when(k < co_n - 1)
                def _():
                    fetch(far(k + 1) * ci_n + lax.rem(ci + 1, ci_n), ahead % 2).start()
            fetch(j, slot).wait()
            part = dot(s["tile"][slot], s["proj"][...].reshape(span, width), NN)
            if d:
                s["ysend"][t, d - 1] = part.astype(BF)
                send(
                    s["ysend"].at[t, d - 1], s["yrecv"].at[t, d - 1], s["yss"].at[t, d - 1],
                    s["yrs"].at[t, d - 1], r, co * ci_n + target,
                ).start()
            else:
                s["mine"][t] = part
            s["spread"][j] = dot(s["tile"][slot], s["panel"][...].reshape(span, width), NN).astype(BF)
        return carry

    lax.fori_loop(0, co_n, forward, 0)

    def along(k, carry):
        t = far(k)
        for d in range(1, ci_n):
            arrived(s["yrecv"].at[t, d - 1], s["yrs"].at[t, d - 1], s["yss"].at[t, d - 1])
            s["mine"][t] = s["mine"][t] + s["yrecv"][t, d - 1].astype(F32)

        @pl.when(jnp.logical_and(t >= co, co > 0))
        def _():
            arrived(s["rrecv"].at[t], s["rrs"].at[t], s["lss"].at[t])
            s["mine"][t] = s["mine"][t] + s["rrecv"][t].astype(F32)

        @pl.when(jnp.logical_and(t <= co, co < co_n - 1))
        def _():
            arrived(s["lrecv"].at[t], s["lrs"].at[t], s["lss"].at[t])
            s["mine"][t] = s["mine"][t] + s["lrecv"][t].astype(F32)

        @pl.when(t != co)
        def _():
            s["lsend"][t] = s["mine"][t].astype(BF)

        @pl.when(t > co)
        def _():
            send(s["lsend"].at[t], s["rrecv"].at[t], s["lss"].at[t], s["rrs"].at[t], r, c + ci_n).start()

        @pl.when(t < co)
        def _():
            send(s["lsend"].at[t], s["lrecv"].at[t], s["lss"].at[t], s["lrs"].at[t], r, c - ci_n).start()

        return carry

    lax.fori_loop(0, co_n, along, 0)

    pre = s["mine"][co]
    sig = jax.nn.sigmoid(pre)
    s["up"][c] = (cot[...].astype(F32) * sig * (1.0 + pre * (1.0 - sig))).astype(BF)

    s["back"][...] = jnp.zeros(s["back"].shape, F32)
    s["gw"][...] = jnp.zeros(s["gw"].shape, F32)

    def upcopy(slot, kind, row, col):
        return send(s["up"].at[slot], s["up"].at[slot], s["uss"].at[slot, kind], s["urs"].at[slot], row, col)

    def use(j):
        fetch(j, 0).wait()
        u = s["up"][j]

        def piece(q, carry):
            cols = pl.ds(pl.multiple_of(q * rows, rows), rows)
            s["back"][q] = s["back"][q] + dot(s["tile"][0, :, cols], u, TN)
            return carry

        lax.fori_loop(0, n_row, piece, 0)
        s["gw"][...] = s["gw"][...] + dot(s["spread"][j], u, TN)

    def collect(j):
        fetch(j, 0).start()
        arrived(s["up"].at[j], s["urs"].at[j], s["uss"].at[j, 0])
        use(j)

    def backward(k, carry):
        t = far(co_n - 1 - k)
        j = t * ci_n + ci
        fetch(j, 0).start()

        @pl.when(k > 0)
        def _():
            arrived(s["up"].at[j], s["urs"].at[j], s["uss"].at[j, 0])

        @pl.when(jnp.logical_and(t <= co, co < co_n - 1))
        def _():
            upcopy(j, 0, r, c + ci_n).start()

        @pl.when(jnp.logical_and(t >= co, co > 0))
        def _():
            upcopy(j, 1, r, c - ci_n).start()

        for d in range(1, ci_n):
            upcopy(j, 1 + d, r, co * ci_n + lax.rem(ci + d, ci_n)).start()

        @pl.when(k == 0)
        def _():
            value = s["mine"][co]
            out[...] = (value * jax.nn.sigmoid(value)).astype(BF)

        use(j)

        @pl.when(k > 0)
        def _():
            before = far(co_n - k)
            for d in range(1, ci_n):
                collect(before * ci_n + lax.rem(ci + d, ci_n))

        return carry

    lax.fori_loop(0, co_n, backward, 0)
    for d in range(1, ci_n):
        collect(far(0) * ci_n + lax.rem(ci + d, ci_n))

    height = width // n_row
    s["gsend"][...] = s["gw"][...].astype(BF).reshape(n_row, height, width)
    for d in range(1, n_row):
        peer = lax.rem(r + d, n_row)
        cp = send(s["gsend"].at[peer], s["grecv"].at[d - 1], s["gss"].at[d - 1], s["grs"].at[d - 1], peer, c)
        cp.start()
        pending.append(cp)

    for q in range(ro_n):
        d = lax.rem(ro + 1 + q, ro_n)
        s["bsend"][d] = s["back"][d * ri_n + (1 - ri)].astype(BF)
        cp = send(s["bsend"].at[d], s["brecv"].at[d], s["bss"].at[d], s["brs"].at[d], mate, c)
        cp.start()
        pending.append(cp)
    for q in range(1, ro_n):
        d = lax.rem(ro + q, ro_n)
        arrived(s["brecv"].at[d], s["brs"].at[d], s["bss"].at[d])
        s["xsend"][q - 1] = (s["back"][d * ri_n + ri] + s["brecv"][d].astype(F32)).astype(BF)
        cp = send(
            s["xsend"].at[q - 1], s["xrecv"].at[q - 1], s["xss"].at[q - 1], s["xrs"].at[q - 1], d * ri_n + ri, c
        )
        cp.start()
        pending.append(cp)
    arrived(s["brecv"].at[ro], s["brs"].at[ro], s["bss"].at[ro])

    groups = s["part"].shape[0]
    thin = s["part"].shape[1]
    total = s["gsend"][r].astype(F32)
    for d in range(1, n_row):
        arrived(s["grecv"].at[d - 1], s["grs"].at[d - 1], s["gss"].at[d - 1])
        total = total + s["grecv"][d - 1].astype(F32)
    s["part"][...] = total.astype(BF).reshape(groups, thin, width)
    own = c % groups
    for d in range(1, n_col):
        peer = lax.rem(c + d, n_col)
        cp = send(s["part"].at[peer % groups], s["crecv"].at[c], s["css"].at[d - 1], s["crs"].at[c], r, peer)
        cp.start()
        pending.append(cp)
    s["crecv"][c] = s["part"][own]

    grad = s["back"][r] + s["brecv"][ro].astype(F32)
    for q in range(1, ro_n):
        arrived(s["xrecv"].at[q - 1], s["xrs"].at[q - 1], s["xss"].at[q - 1])
        grad = grad + s["xrecv"][q - 1].astype(F32)
    gfeat[...] = dot(grad.astype(BF), weight[...], NT).astype(BF)

    for d in range(1, n_col):
        slot = lax.rem(c + d, n_col)
        arrived(s["crecv"].at[slot], s["crs"].at[slot], s["css"].at[0])
    total = s["crecv"][0].astype(F32)
    for q in range(1, n_col):
        total = total + s["crecv"][q].astype(F32)
    place = pl.ds(pl.multiple_of(own * thin, thin), thin)
    s["full"][r, place, :] = total.astype(BF)
    for d in range(1, groups):
        peer = (c // groups) * groups + lax.rem(own + d, groups)
        cp = send(
            s["full"].at[r, place, :], s["full"].at[r, place, :], s["dss"].at[d], s["drs"].at[own], r, peer
        )
        cp.start()
        pending.append(cp)
    for d in range(1, groups):
        slot = lax.rem(own + d, groups)
        arrived(
            s["full"].at[r, pl.ds(pl.multiple_of(slot * thin, thin), thin), :], s["drs"].at[slot], s["dss"].at[0]
        )
    for d in range(1, n_row):
        cp = send(s["full"].at[r], s["full"].at[r], s["ess"].at[d], s["ers"].at[r], lax.rem(r + d, n_row), c)
        cp.start()
        pending.append(cp)
    for d in range(1, n_row):
        slot = lax.rem(r + d, n_row)
        arrived(s["full"].at[slot], s["ers"].at[slot], s["ess"].at[0])
    gweight[...] = s["full"][...].reshape(width, width).astype(F32)

    def left(k, carry):
        for d in range(1, ci_n):
            send(
                s["ysend"].at[k, d - 1], s["yrecv"].at[k, d - 1], s["yss"].at[k, d - 1], s["yrs"].at[k, d - 1],
                r, lax.rem(c + 1, n_col),
            ).wait_send()
            upcopy(k * ci_n + ci, 1 + d, r, lax.rem(c + 1, n_col)).wait_send()

        @pl.when(k != co)
        def _():
            send(s["lsend"].at[k], s["rrecv"].at[k], s["lss"].at[k], s["rrs"].at[k], r, lax.rem(c + 1, n_col)).wait_send()

        @pl.when(jnp.logical_and(k <= co, co < co_n - 1))
        def _():
            upcopy(k * ci_n + ci, 0, r, lax.rem(c + 1, n_col)).wait_send()

        @pl.when(jnp.logical_and(k >= co, co > 0))
        def _():
            upcopy(k * ci_n + ci, 1, r, lax.rem(c + 1, n_col)).wait_send()

        return carry

    lax.fori_loop(0, co_n, left, 0)
    for cp in pending:
        cp.wait_send()


def solution(mesh):
    n_row, n_col = mesh.shape["row"], mesh.shape["col"]

    def shards(features, weight, entry_values, block_rows, block_cols, entry_counts, cotangent):
        rows, width = features.shape
        span = n_row * rows
        co_n, ci_n, ro_n = 4, n_col // 4, n_row // 2
        smem = pl.BlockSpec(memory_space=pltpu.SMEM)
        vmem = pl.BlockSpec(memory_space=pltpu.VMEM)
        dense = pl.pallas_call(
            densify,
            out_shape=jax.ShapeDtypeStruct((n_col, rows, span), BF),
            in_specs=[vmem, smem, smem, smem],
            out_specs=vmem,
            compiler_params=pltpu.CompilerParams(vmem_limit_bytes=VMEM_LIMIT),
        )(entry_values[0, 0], block_rows[0, 0], block_cols[0, 0], entry_counts[0])

        height = width // n_row
        groups = min(n_col, height // 16)
        thin = height // groups
        block = (rows, width)
        sem = pltpu.SemaphoreType.DMA
        scratch = {
            "panel": pltpu.VMEM((n_row,) + block, BF),
            "proj": pltpu.VMEM((n_row,) + block, BF),
            "pss": sem((2 * ro_n,)),
            "prs": sem((n_row,)),
            "tile": pltpu.VMEM((2, rows, span), BF),
            "ts": sem((2,)),
            "ysend": pltpu.VMEM((co_n, ci_n - 1) + block, BF),
            "yrecv": pltpu.VMEM((co_n, ci_n - 1) + block, BF),
            "yss": sem((co_n, ci_n - 1)),
            "yrs": sem((co_n, ci_n - 1)),
            "mine": pltpu.VMEM((co_n,) + block, F32),
            "spread": pltpu.VMEM((n_col,) + block, BF),
            "lsend": pltpu.VMEM((co_n,) + block, BF),
            "rrecv": pltpu.VMEM((co_n,) + block, BF),
            "lrecv": pltpu.VMEM((co_n,) + block, BF),
            "lss": sem((co_n,)),
            "rrs": sem((co_n,)),
            "lrs": sem((co_n,)),
            "up": pltpu.VMEM((n_col,) + block, BF),
            "uss": sem((n_col, ci_n + 1)),
            "urs": sem((n_col,)),
            "back": pltpu.VMEM((n_row,) + block, F32),
            "gw": pltpu.VMEM((width, width), F32),
            "gsend": pltpu.VMEM((n_row, height, width), BF),
            "grecv": pltpu.VMEM((n_row - 1, height, width), BF),
            "gss": sem((n_row - 1,)),
            "grs": sem((n_row - 1,)),
            "bsend": pltpu.VMEM((ro_n,) + block, BF),
            "brecv": pltpu.VMEM((ro_n,) + block, BF),
            "bss": sem((ro_n,)),
            "brs": sem((ro_n,)),
            "xsend": pltpu.VMEM((ro_n - 1,) + block, BF),
            "xrecv": pltpu.VMEM((ro_n - 1,) + block, BF),
            "xss": sem((ro_n - 1,)),
            "xrs": sem((ro_n - 1,)),
            "part": pltpu.VMEM((groups, thin, width), BF),
            "crecv": pltpu.VMEM((n_col, thin, width), BF),
            "css": sem((n_col - 1,)),
            "crs": sem((n_col,)),
            "full": pltpu.VMEM((n_row, height, width), BF),
            "dss": sem((groups,)),
            "drs": sem((groups,)),
            "ess": sem((n_row,)),
            "ers": sem((n_row,)),
        }
        names = list(scratch)

        def kernel(feat, w, a, cot, out, gfeat, gweight, *refs):
            layer(n_row, n_col, feat, w, a, cot, out, gfeat, gweight, dict(zip(names, refs)))

        return tuple(
            pl.pallas_call(
                kernel,
                out_shape=(
                    jax.ShapeDtypeStruct(block, BF),
                    jax.ShapeDtypeStruct(block, BF),
                    jax.ShapeDtypeStruct((width, width), F32),
                ),
                in_specs=[vmem, vmem, pl.BlockSpec(memory_space=pl.ANY), vmem],
                out_specs=(vmem, vmem, vmem),
                scratch_shapes=[scratch[name] for name in names],
                compiler_params=pltpu.CompilerParams(
                    collective_id=0, has_side_effects=True, vmem_limit_bytes=VMEM_LIMIT
                ),
            )(features, weight, dense, cotangent)
        )

    return jax.shard_map(
        shards,
        mesh=mesh,
        in_specs=(
            P(("col", "row"), None),
            P(),
            P("row", "col", None, None, None),
            P("row", "col", None),
            P("row", "col", None),
            P("row", "col"),
            P(("row", "col"), None),
        ),
        out_specs=(P(("row", "col"), None), P(("col", "row"), None), P()),
        check_vma=False,
    )
```

time: 434 us -> 112 us (0.26)
  waiting for transfers between devices: 326 us -> 0 us
  Pallas kernels: 0 us -> 103 us
  other arithmetic: 42.2 us -> 0 us
  local copies, waits for them, and re-layouts: 30.1 us -> 5.6 us
  matrix products: 19.8 us -> 0 us
  between operations: 14.5 us -> 1.29 us
    psum x2 -> x0, waiting for transfers between devices: 233 us -> none  [the longest x1 131 us: shards(): grad_weight = lax.psum(weight_term, ('row', 'col'))]
    pallas_call x0 -> x2, Pallas kernels: none -> 103 us  [the longest x1 98.9 us: shards(): pl.pallas_call(kernel, out_shape=(jax.ShapeDtypeStruct(block, BF), jax.Sh...]
    all_gather x2 -> x0, waiting for transfers between devices: 68.7 us -> none  [the longest x1 51.2 us: shards(): incoming = lax.all_gather(cotangent, 'col', axis=0, tiled=True)]
    scatter-add x2 -> x0, other arithmetic: 29.9 us -> none  [one_group(): return running.at[target_ids].add(products * alive_mask[:, None, None])]
    reduce_scatter x1 -> x0, waiting for transfers between devices: 23.5 us -> none  [shards(): lax.psum_scatter(backward_terms.astype(jnp.bfloat16), 'row', scatter_dime...]
    dot_general x5 -> x0, matrix products: 19.8 us -> none  [the longest x1 7.15 us: one_group(): jnp.einsum('kba,kbf->kaf', values, tiles, preferred_element_type=jnp.floa...]
    mul x2 -> x0, local copies, waits for them, and re-layouts: 18 us -> none  [one_group(): return running.at[target_ids].add(products * alive_mask[:, None, None])]
    convert_element_type x6 -> x0, other arithmetic: 11 us -> none  [the longest x1 3.93 us: shards(): (incoming.astype(jnp.float32) * silu_slope(summed)).astype(jnp.bfloat16)]
  transfers between devices with their start and end apart: 5 -> 0, of which waited for: 5 -> 0; matrix products, arithmetic and copies ran while one was open for 1% -> 0% of each run, Pallas kernels for 0% -> 0%
where the time goes in v1:
time: 112 us; the launch traced here: 110 us
  Pallas kernels  103 us (92%)
  local copies, waits for them, and re-layouts  5.6 us (5%)
  between operations  1.29 us (1%)
    pallas_call x1, Pallas kernels, shards(): pl.pallas_call(kernel, out_shape=(jax.ShapeDtypeStruct(block, BF), jax.Sh...  98.9 us
    unnamed x3, local copies, waits for them, and re-layouts  5.6 us
    pallas_call x1, Pallas kernels, shards(): pl.pallas_call(densify, out_shape=jax.ShapeDtypeStruct((n_col, rows, span...  4.01 us

profile of v1, /device:TPU:0, one launch (start us, length us, event | category | flops | bytes accessed | tf_op | source)
XLA Modules:
  0.0 109.8 jit_solution(12552573520521699110)
XLA Ops:
  1.3 4.0 %shard_map.94.a = bf16[8,256,1024]{2,1,0:T(8,128)(2,1)} custom-call(bf16[32,128,128]{2,1,0:T(8,128)(2,1)} %bitcast.5, s32[32]{0:T(128)} %bitcast.6, s32[32]{0:T(128)} %bitcast.7, s32[1]{0:T(128)} %bitcast.4.count), custom_call_target="tpu_custom_call" | custom-call | tf_op jit(solution)/shard_map/pallas_call | solution.py:360
  5.3 98.9 %shard_map.95 = (bf16[256,512]{1,0:T(8,128)(2,1)}, bf16[256,512]{1,0:T(8,128)(2,1)}, f32[512,512]{1,0:T(8,128)}) custom-call(bf16[256,512]{1,0:T(8,128)(2,1)} %feat.1, bf16[512,512]{1,0:T(8,128)(2,1)} %w.1, bf16[8,256,1024]{2,1,0:T(8,128)(2,1)} %shard_map.94.a, bf16[256,512]{1,0:T(8,128)(2,1)} %cot.1), custom_call_target="tpu_custom_call" | custom-call | tf_op jit(solution)/shard_map/pallas_call | solution.py:425
  104.2 1.7 %copy.14 = bf16[256,512]{1,0:T(8,128)(2,1)} copy(bf16[256,512]{1,0:T(8,128)(2,1)} %get-tuple-element.6) | data formatting | bytes 524288
  105.8 1.7 %copy.15 = bf16[256,512]{1,0:T(8,128)(2,1)} copy(bf16[256,512]{1,0:T(8,128)(2,1)} %get-tuple-element.7) | data formatting | bytes 524288
  107.5 2.3 %copy.16 = f32[512,512]{1,0:T(8,128)} copy(f32[512,512]{1,0:T(8,128)} %get-tuple-element.8) | data formatting | bytes 2097152

commit v2 on v1

--- a/solution.py
+++ b/solution.py
@@ -11,6 +11,7 @@
 BF = jnp.bfloat16
 F32 = jnp.float32
 VMEM_LIMIT = 60 * 1024 * 1024
+PIECES = 2
 
 
 def densify(values, rows, cols, count, dense):
@@ -45,7 +46,13 @@
 NT = ((1,), (1,))
 
 
-def layer(n_row, n_col, feat, weight, dense, cot, out, gfeat, gweight, s):
+def finish(out_in, gfeat_in, gweight_in, out, gfeat, gweight):
+    out[...] = out_in[...]
+    gfeat[...] = gfeat_in[...]
+    gweight[...] = gweight_in[...].astype(F32)
+
+
+def layer(n_row, n_col, feat, weight_in, dense, cot_in, out, gfeat, gweight, s):
     ri_n = 2
     ro_n = n_row // ri_n
     co_n = 4
@@ -55,6 +62,9 @@
     ro, ri = r // ri_n, r % ri_n
     co, ci = c // ci_n, c % ci_n
     span = n_row * rows
+    thick = rows // PIECES
+    cuts = [pl.ds(h * thick, thick) for h in range(PIECES)]
+    weight, cot = s["weight"], s["cot"]
 
     def send(src, dst, ss, rs, row, col):
         return pltpu.make_async_remote_copy(
@@ -69,6 +79,13 @@
         pl.semaphore_signal(barrier, inc=1, device_id=(lax.rem(r + d, n_row), c), device_id_type=MESH)
     for d in range(1, n_col):
         pl.semaphore_signal(barrier, inc=1, device_id=(r, lax.rem(c + d, n_col)), device_id_type=MESH)
+    loads = [
+        pltpu.make_async_copy(feat, s["panel"].at[r], s["ls"].at[0]),
+        pltpu.make_async_copy(weight_in, weight, s["ls"].at[1]),
+        pltpu.make_async_copy(cot_in, cot, s["ls"].at[2]),
+    ]
+    for cp in loads:
+        cp.start()
     pl.semaphore_wait(barrier, n_row + n_col - 2)
 
     mate = ro * ri_n + (1 - ri)
@@ -81,7 +98,27 @@
     cp = send(feat, s["panel"].at[r], s["pss"].at[ro_n - 1], s["prs"].at[r], mate, c)
     cp.start()
     pending.append(cp)
-    s["panel"][r] = feat[...]
+
+    def far(k):
+        table = ((3, 2, 1, 0), (3, 0, 2, 1), (0, 3, 1, 2), (0, 1, 2, 3))
+
+        def entry(pos):
+            picked = jnp.int32(table[pos][co_n - 1])
+            for q in range(co_n - 1):
+                picked = jnp.where(k == q, table[pos][q], picked)
+            return picked
+
+        picked = entry(co_n - 1)
+        for pos in range(co_n - 1):
+            picked = jnp.where(co == pos, entry(pos), picked)
+        return picked
+
+    def fetch(j, slot):
+        return pltpu.make_async_copy(dense.at[j], s["tile"].at[slot], s["ts"].at[slot])
+
+    fetch(far(0) * ci_n + lax.rem(ci + 1, ci_n), 0).start()
+    for cp in loads:
+        cp.wait()
 
     def project(slot):
         s["proj"][slot] = dot(s["panel"][slot], weight[...], NN).astype(BF)
@@ -99,24 +136,19 @@
         arrived(s["panel"].at[slot], s["prs"].at[slot], s["pss"].at[0])
         project(slot)
 
-    def far(k):
-        table = ((3, 2, 1, 0), (3, 0, 2, 1), (0, 3, 1, 2), (0, 1, 2, 3))
-
-        def entry(pos):
-            picked = jnp.int32(table[pos][co_n - 1])
-            for q in range(co_n - 1):
-                picked = jnp.where(k == q, table[pos][q], picked)
-            return picked
-
-        picked = entry(co_n - 1)
-        for pos in range(co_n - 1):
-            picked = jnp.where(co == pos, entry(pos), picked)
-        return picked
-
-    def fetch(j, slot):
-        return pltpu.make_async_copy(dense.at[j], s["tile"].at[slot], s["ts"].at[slot])
-
-    fetch(far(0) * ci_n + lax.rem(ci + 1, ci_n), 0).start()
+    def ycopy(t, d, h, col):
+        return send(
+            s["ysend"].at[t, d, cuts[h]], s["yrecv"].at[t, d, cuts[h]], s["yss"].at[t, d, h], s["yrs"].at[t, d, h],
+            r, col,
+        )
+
+    def lcopy(t, h, name, col):
+        return send(
+            s["lsend"].at[t, cuts[h]], s[name + "recv"].at[t, cuts[h]], s["lss"].at[t, h], s[name + "rs"].at[t, h],
+            r, col,
+        )
+
+    other = lax.rem(c + 1, n_col)
 
     def forward(k, carry):
         t = far(k)
@@ -137,10 +169,8 @@
             part = dot(s["tile"][slot], s["proj"][...].reshape(span, width), NN)
             if d:
                 s["ysend"][t, d - 1] = part.astype(BF)
-                send(
-                    s["ysend"].at[t, d - 1], s["yrecv"].at[t, d - 1], s["yss"].at[t, d - 1],
-                    s["yrs"].at[t, d - 1], r, co * ci_n + target,
-                ).start()
+                for h in range(PIECES):
+                    ycopy(t, d - 1, h, co * ci_n + target).start()
             else:
                 s["mine"][t] = part
             s["spread"][j] = dot(s["tile"][slot], s["panel"][...].reshape(span, width), NN).astype(BF)
@@ -150,31 +180,33 @@
 
     def along(k, carry):
         t = far(k)
-        for d in range(1, ci_n):
-            arrived(s["yrecv"].at[t, d - 1], s["yrs"].at[t, d - 1], s["yss"].at[t, d - 1])
-            s["mine"][t] = s["mine"][t] + s["yrecv"][t, d - 1].astype(F32)
-
-        @pl.when(jnp.logical_and(t >= co, co > 0))
-        def _():
-            arrived(s["rrecv"].at[t], s["rrs"].at[t], s["lss"].at[t])
-            s["mine"][t] = s["mine"][t] + s["rrecv"][t].astype(F32)
-
-        @pl.when(jnp.logical_and(t <= co, co < co_n - 1))
-        def _():
-            arrived(s["lrecv"].at[t], s["lrs"].at[t], s["lss"].at[t])
-            s["mine"][t] = s["mine"][t] + s["lrecv"][t].astype(F32)
-
-        @pl.when(t != co)
-        def _():
-            s["lsend"][t] = s["mine"][t].astype(BF)
-
-        @pl.when(t > co)
-        def _():
-            send(s["lsend"].at[t], s["rrecv"].at[t], s["lss"].at[t], s["rrs"].at[t], r, c + ci_n).start()
-
-        @pl.when(t < co)
-        def _():
-            send(s["lsend"].at[t], s["lrecv"].at[t], s["lss"].at[t], s["lrs"].at[t], r, c - ci_n).start()
+        for h in range(PIECES):
+            cut = cuts[h]
+            for d in range(1, ci_n):
+                ycopy(t, d - 1, h, other).wait_recv()
+                s["mine"][t, cut] = s["mine"][t, cut] + s["yrecv"][t, d - 1, cut].astype(F32)
+
+            @pl.when(jnp.logical_and(t >= co, co > 0))
+            def _():
+                lcopy(t, h, "r", other).wait_recv()
+                s["mine"][t, cut] = s["mine"][t, cut] + s["rrecv"][t, cut].astype(F32)
+
+            @pl.when(jnp.logical_and(t <= co, co < co_n - 1))
+            def _():
+                lcopy(t, h, "l", other).wait_recv()
+                s["mine"][t, cut] = s["mine"][t, cut] + s["lrecv"][t, cut].astype(F32)
+
+            @pl.when(t != co)
+            def _():
+                s["lsend"][t, cut] = s["mine"][t, cut].astype(BF)
+
+            @pl.when(t > co)
+            def _():
+                lcopy(t, h, "r", c + ci_n).start()
+
+            @pl.when(t < co)
+            def _():
+                lcopy(t, h, "l", c - ci_n).start()
 
         return carry
 
@@ -187,64 +219,104 @@
     s["back"][...] = jnp.zeros(s["back"].shape, F32)
     s["gw"][...] = jnp.zeros(s["gw"].shape, F32)
 
-    def upcopy(slot, kind, row, col):
-        return send(s["up"].at[slot], s["up"].at[slot], s["uss"].at[slot, kind], s["urs"].at[slot], row, col)
-
-    def use(j):
-        fetch(j, 0).wait()
+    def upcopy(slot, h, kind, row, col):
+        return send(
+            s["up"].at[slot, cuts[h]], s["up"].at[slot, cuts[h]], s["uss"].at[slot, h, kind], s["urs"].at[slot, h],
+            row, col,
+        )
+
+    def use_back(j, slot):
+        fetch(j, slot).wait()
         u = s["up"][j]
 
         def piece(q, carry):
             cols = pl.ds(pl.multiple_of(q * rows, rows), rows)
-            s["back"][q] = s["back"][q] + dot(s["tile"][0, :, cols], u, TN)
+            s["back"][q] = s["back"][q] + dot(s["tile"][slot, :, cols], u, TN)
             return carry
 
         lax.fori_loop(0, n_row, piece, 0)
-        s["gw"][...] = s["gw"][...] + dot(s["spread"][j], u, TN)
-
-    def collect(j):
-        fetch(j, 0).start()
-        arrived(s["up"].at[j], s["urs"].at[j], s["uss"].at[j, 0])
-        use(j)
-
-    def backward(k, carry):
+
+    def use_gw(j):
+        s["gw"][...] = s["gw"][...] + dot(s["spread"][j], s["up"][j], TN)
+
+    def wait_up(j):
+        for h in range(PIECES):
+            upcopy(j, h, 0, r, other).wait_recv()
+
+    def pass_on(k, h):
         t = far(co_n - 1 - k)
         j = t * ci_n + ci
-        fetch(j, 0).start()
 
         @pl.when(k > 0)
         def _():
-            arrived(s["up"].at[j], s["urs"].at[j], s["uss"].at[j, 0])
+            upcopy(j, h, 0, r, other).wait_recv()
 
         @pl.when(jnp.logical_and(t <= co, co < co_n - 1))
         def _():
-            upcopy(j, 0, r, c + ci_n).start()
+            upcopy(j, h, 0, r, c + ci_n).start()
 
         @pl.when(jnp.logical_and(t >= co, co > 0))
         def _():
-            upcopy(j, 1, r, c - ci_n).start()
+            upcopy(j, h, 1, r, c - ci_n).start()
 
         for d in range(1, ci_n):
-            upcopy(j, 1 + d, r, co * ci_n + lax.rem(ci + d, ci_n)).start()
+            upcopy(j, h, 1 + d, r, co * ci_n + lax.rem(ci + d, ci_n)).start()
+
+    def own_chunk(k):
+        return far(co_n - 1 - k) * ci_n + ci
+
+    def side_chunk(k, d):
+        return far(co_n - 1 - k) * ci_n + lax.rem(ci + d, ci_n)
+
+    def use_own(k):
+        j = own_chunk(k)
+        use_back(j, 0)
+        use_gw(j)
+
+    def use_sides(k):
+        for d in range(1, ci_n):
+            j = side_chunk(k, d)
+            fetch(j, 1).start()
+            wait_up(j)
+            use_back(j, 1)
+            use_gw(j)
+
+    def backward(k, carry):
+        @pl.when(k > 0)
+        def _():
+            fetch(own_chunk(k - 1), 0).start()
+
+        for h in range(PIECES - 1):
+            pass_on(k, h)
+
+        @pl.when(k > 0)
+        def _():
+            use_own(k - 1)
+
+        pass_on(k, PIECES - 1)
 
         @pl.when(k == 0)
         def _():
             value = s["mine"][co]
             out[...] = (value * jax.nn.sigmoid(value)).astype(BF)
 
-        use(j)
-
-        @pl.when(k > 0)
-        def _():
-            before = far(co_n - k)
-            for d in range(1, ci_n):
-                collect(before * ci_n + lax.rem(ci + d, ci_n))
+        @pl.when(k > 1)
+        def _():
+            use_sides(k - 2)
 
         return carry
 
     lax.fori_loop(0, co_n, backward, 0)
+    fetch(own_chunk(co_n - 1), 0).start()
+    use_own(co_n - 1)
+    use_sides(co_n - 2)
     for d in range(1, ci_n):
-        collect(far(0) * ci_n + lax.rem(ci + d, ci_n))
+        last = side_chunk(co_n - 1, d)
+        fetch(last, 1).start()
+        wait_up(last)
+        if d < ci_n - 1:
+            use_back(last, 1)
+        use_gw(last)
 
     height = width // n_row
     s["gsend"][...] = s["gw"][...].astype(BF).reshape(n_row, height, width)
@@ -253,6 +325,8 @@
         cp = send(s["gsend"].at[peer], s["grecv"].at[d - 1], s["gss"].at[d - 1], s["grs"].at[d - 1], peer, c)
         cp.start()
         pending.append(cp)
+
+    use_back(last, 1)
 
     for q in range(ro_n):
         d = lax.rem(ro + 1 + q, ro_n)
@@ -300,46 +374,51 @@
         total = total + s["crecv"][q].astype(F32)
     place = pl.ds(pl.multiple_of(own * thin, thin), thin)
     s["full"][r, place, :] = total.astype(BF)
+    def strip(row, piece):
+        return s["full"].at[row, pl.ds(pl.multiple_of(piece * thin, thin), thin), :]
+
+    def spread_rows(piece):
+        for d in range(1, n_row):
+            peer = lax.rem(r + d, n_row)
+            ref = strip(r, piece)
+            cp = send(ref, ref, s["ess"].at[d, piece], s["ers"].at[r, piece], peer, c)
+            cp.start()
+            pending.append(cp)
+
     for d in range(1, groups):
         peer = (c // groups) * groups + lax.rem(own + d, groups)
-        cp = send(
-            s["full"].at[r, place, :], s["full"].at[r, place, :], s["dss"].at[d], s["drs"].at[own], r, peer
-        )
-        cp.start()
-        pending.append(cp)
+        cp = send(strip(r, own), strip(r, own), s["dss"].at[d], s["drs"].at[own], r, peer)
+        cp.start()
+        pending.append(cp)
+    spread_rows(own)
     for d in range(1, groups):
-        slot = lax.rem(own + d, groups)
-        arrived(
-            s["full"].at[r, pl.ds(pl.multiple_of(slot * thin, thin), thin), :], s["drs"].at[slot], s["dss"].at[0]
-        )
+        slot = lax.rem(own + groups - d, groups)
+        arrived(strip(r, slot), s["drs"].at[slot], s["dss"].at[0])
+        spread_rows(slot)
     for d in range(1, n_row):
-        cp = send(s["full"].at[r], s["full"].at[r], s["ess"].at[d], s["ers"].at[r], lax.rem(r + d, n_row), c)
-        cp.start()
-        pending.append(cp)
-    for d in range(1, n_row):
-        slot = lax.rem(r + d, n_row)
-        arrived(s["full"].at[slot], s["ers"].at[slot], s["ess"].at[0])
-    gweight[...] = s["full"][...].reshape(width, width).astype(F32)
+        row = lax.rem(r + d, n_row)
+        for piece in range(groups):
+            arrived(strip(row, piece), s["ers"].at[row, piece], s["ess"].at[0, 0])
+    gweight[...] = s["full"][...].reshape(width, width)
 
     def left(k, carry):
-        for d in range(1, ci_n):
-            send(
-                s["ysend"].at[k, d - 1], s["yrecv"].at[k, d - 1], s["yss"].at[k, d - 1], s["yrs"].at[k, d - 1],
-                r, lax.rem(c + 1, n_col),
-            ).wait_send()
-            upcopy(k * ci_n + ci, 1 + d, r, lax.rem(c + 1, n_col)).wait_send()
-
-        @pl.when(k != co)
-        def _():
-            send(s["lsend"].at[k], s["rrecv"].at[k], s["lss"].at[k], s["rrs"].at[k], r, lax.rem(c + 1, n_col)).wait_send()
-
-        @pl.when(jnp.logical_and(k <= co, co < co_n - 1))
-        def _():
-            upcopy(k * ci_n + ci, 0, r, lax.rem(c + 1, n_col)).wait_send()
-
-        @pl.when(jnp.logical_and(k >= co, co > 0))
-        def _():
-            upcopy(k * ci_n + ci, 1, r, lax.rem(c + 1, n_col)).wait_send()
+        j = k * ci_n + ci
+        for h in range(PIECES):
+            for d in range(1, ci_n):
+                ycopy(k, d - 1, h, other).wait_send()
+                upcopy(j, h, 1 + d, r, other).wait_send()
+
+            @pl.when(k != co)
+            def _():
+                lcopy(k, h, "r", other).wait_send()
+
+            @pl.when(jnp.logical_and(k <= co, co < co_n - 1))
+            def _():
+                upcopy(j, h, 0, r, other).wait_send()
+
+            @pl.when(jnp.logical_and(k >= co, co > 0))
+            def _():
+                upcopy(j, h, 1, r, other).wait_send()
 
         return carry
 
@@ -375,23 +454,26 @@
             "proj": pltpu.VMEM((n_row,) + block, BF),
             "pss": sem((2 * ro_n,)),
             "prs": sem((n_row,)),
+            "weight": pltpu.VMEM((width, width), BF),
+            "cot": pltpu.VMEM(block, BF),
+            "ls": sem((3,)),
             "tile": pltpu.VMEM((2, rows, span), BF),
             "ts": sem((2,)),
             "ysend": pltpu.VMEM((co_n, ci_n - 1) + block, BF),
             "yrecv": pltpu.VMEM((co_n, ci_n - 1) + block, BF),
-            "yss": sem((co_n, ci_n - 1)),
-            "yrs": sem((co_n, ci_n - 1)),
+            "yss": sem((co_n, ci_n - 1, PIECES)),
+            "yrs": sem((co_n, ci_n - 1, PIECES)),
             "mine": pltpu.VMEM((co_n,) + block, F32),
             "spread": pltpu.VMEM((n_col,) + block, BF),
             "lsend": pltpu.VMEM((co_n,) + block, BF),
             "rrecv": pltpu.VMEM((co_n,) + block, BF),
             "lrecv": pltpu.VMEM((co_n,) + block, BF),
-            "lss": sem((co_n,)),
-            "rrs": sem((co_n,)),
-            "lrs": sem((co_n,)),
+            "lss": sem((co_n, PIECES)),
+            "rrs": sem((co_n, PIECES)),
+            "lrs": sem((co_n, PIECES)),
             "up": pltpu.VMEM((n_col,) + block, BF),
-            "uss": sem((n_col, ci_n + 1)),
-            "urs": sem((n_col,)),
+            "uss": sem((n_col, PIECES, ci_n + 1)),
+            "urs": sem((n_col, PIECES)),
             "back": pltpu.VMEM((n_row,) + block, F32),
             "gw": pltpu.VMEM((width, width), F32),
             "gsend": pltpu.VMEM((n_row, height, width), BF),
@@ -413,29 +495,36 @@
             "full": pltpu.VMEM((n_row, height, width), BF),
             "dss": sem((groups,)),
             "drs": sem((groups,)),
-            "ess": sem((n_row,)),
-            "ers": sem((n_row,)),
+            "ess": sem((n_row, groups)),
+            "ers": sem((n_row, groups)),
         }
         names = list(scratch)
 
         def kernel(feat, w, a, cot, out, gfeat, gweight, *refs):
             layer(n_row, n_col, feat, w, a, cot, out, gfeat, gweight, dict(zip(names, refs)))
 
+        def shapes(kind):
+            return (
+                jax.ShapeDtypeStruct(block, BF),
+                jax.ShapeDtypeStruct(block, BF),
+                jax.ShapeDtypeStruct((width, width), kind),
+            )
+
+        free = pl.BlockSpec(memory_space=pl.ANY)
+        results = pl.pallas_call(
+            kernel,
+            out_shape=shapes(BF),
+            in_specs=[free, free, free, free],
+            out_specs=(vmem, vmem, vmem),
+            scratch_shapes=[scratch[name] for name in names],
+            compiler_params=pltpu.CompilerParams(
+                collective_id=0, has_side_effects=True, vmem_limit_bytes=VMEM_LIMIT
+            ),
+        )(features, weight, dense, cotangent)
         return tuple(
             pl.pallas_call(
-                kernel,
-                out_shape=(
-                    jax.ShapeDtypeStruct(block, BF),
-                    jax.ShapeDtypeStruct(block, BF),
-                    jax.ShapeDtypeStruct((width, width), F32),
-                ),
-                in_specs=[vmem, vmem, pl.BlockSpec(memory_space=pl.ANY), vmem],
-                out_specs=(vmem, vmem, vmem),
-                scratch_shapes=[scratch[name] for name in names],
-                compiler_params=pltpu.CompilerParams(
-                    collective_id=0, has_side_effects=True, vmem_limit_bytes=VMEM_LIMIT
-                ),
-            )(features, weight, dense, cotangent)
+                finish, out_shape=shapes(F32), in_specs=[vmem] * 3, out_specs=(vmem, vmem, vmem)
+            )(*results)
         )
 
     return jax.shard_map(

time: 112 us -> 102 us (0.911); the launches traced: 110 us -> 101 us
  local copies, waits for them, and re-layouts: 5.6 us -> 0 us
  Pallas kernels: 103 us -> 99.7 us
    unnamed x3 -> x0, local copies, waits for them, and re-layouts: 5.6 us -> none
    pallas_call x1 -> x2, Pallas kernels: 98.9 us -> 95.7 us  [the longest x1 93.3 us: shards(): pl.pallas_call(kernel, out_shape=shapes(BF), in_specs=[free, free, free,...]
where the time goes in v2:
time: 102 us; the launch traced here: 101 us
  Pallas kernels  99.7 us (98%)
  between operations  1.29 us (1%)
    pallas_call x1, Pallas kernels, shards(): pl.pallas_call(kernel, out_shape=shapes(BF), in_specs=[free, free, free,...  93.3 us
    pallas_call x1, Pallas kernels, shards(): pl.pallas_call(densify, out_shape=jax.ShapeDtypeStruct((n_col, rows, span...  4.03 us
    pallas_call x1, Pallas kernels, shards(): pl.pallas_call(finish, out_shape=shapes(F32), in_specs=[vmem] * 3, out_sp...  2.36 us

profile of v2, /device:TPU:0, one launch (start us, length us, event | category | flops | bytes accessed | tf_op | source)
XLA Modules:
  0.0 101.0 jit_solution(5823396207899203973)
XLA Ops:
  1.3 4.0 %shard_map.94.a = bf16[8,256,1024]{2,1,0:T(8,128)(2,1)} custom-call(bf16[32,128,128]{2,1,0:T(8,128)(2,1)} %bitcast.5, s32[32]{0:T(128)} %bitcast.6, s32[32]{0:T(128)} %bitcast.7, s32[1]{0:T(128)} %bitcast.4.count), custom_call_target="tpu_custom_call" | custom-call | tf_op jit(solution)/shard_map/pallas_call | solution.py:439
  5.3 93.3 %shard_map.95 = (bf16[256,512]{1,0:T(8,128)(2,1)}, bf16[256,512]{1,0:T(8,128)(2,1)}, bf16[512,512]{1,0:T(8,128)(2,1)}) custom-call(bf16[256,512]{1,0:T(8,128)(2,1)} %feat.1, bf16[512,512]{1,0:T(8,128)(2,1)} %w.1, bf16[8,256,1024]{2,1,0:T(8,128)(2,1)} %shard_map.94.a, bf16[256,512]{1,0:T(8,128)(2,1)} %cot.1), custom_call_target="tpu_custom_call" | custom-call | tf_op jit(solution)/shard_map/pallas_call | solution.py:514
  98.6 2.4 %shard_map.96 = (bf16[256,512]{1,0:T(8,128)(2,1)}, bf16[256,512]{1,0:T(8,128)(2,1)}, f32[512,512]{1,0:T(8,128)}) custom-call(bf16[256,512]{1,0:T(8,128)(2,1)} %get-tuple-element.6.out_in, bf16[256,512]{1,0:T(8,128)(2,1)} %get-tuple-element.7.gfeat_in, bf16[512,512]{1,0:T(8,128)(2,1)} %get-tuple-element.8.gweight_in), custom_call_target="tpu_custom_call" | custom-call | tf_op jit(solution)/shard_map/pallas_call | solution.py:525

commit v3 on v2

--- a/solution.py
+++ b/solution.py
@@ -313,10 +313,31 @@
     for d in range(1, ci_n):
         last = side_chunk(co_n - 1, d)
         fetch(last, 1).start()
-        wait_up(last)
         if d < ci_n - 1:
+            wait_up(last)
             use_back(last, 1)
-        use_gw(last)
+            use_gw(last)
+
+    def back_piece(h):
+        u = s["up"][last, cuts[h]]
+
+        def piece(q, carry):
+            cols = pl.ds(pl.multiple_of(q * rows, rows), rows)
+            s["back"][q] = s["back"][q] + dot(s["tile"][1, cuts[h], cols], u, TN)
+            return carry
+
+        lax.fori_loop(0, n_row, piece, 0)
+
+    def gw_piece(h):
+        s["gw"][...] = s["gw"][...] + dot(s["spread"][last, cuts[h]], s["up"][last, cuts[h]], TN)
+
+    fetch(last, 1).wait()
+    for h in range(PIECES):
+        upcopy(last, h, 0, r, other).wait_recv()
+        gw_piece(h)
+        if h < PIECES - 1:
+            back_piece(h)
+
 
     height = width // n_row
     s["gsend"][...] = s["gw"][...].astype(BF).reshape(n_row, height, width)
@@ -326,7 +347,7 @@
         cp.start()
         pending.append(cp)
 
-    use_back(last, 1)
+    back_piece(PIECES - 1)
 
     for q in range(ro_n):
         d = lax.rem(ro + 1 + q, ro_n)

time: 102 us -> 104 us (1.020); the launches traced: 101 us -> 104 us
  Pallas kernels: 99.7 us -> 103 us
    pallas_call x1, Pallas kernels: 93.3 us -> 96.6 us  [shards(): pl.pallas_call(kernel, out_shape=shapes(BF), in_specs=[free, free, free,...]
where the time goes in v3:
time: 104 us
  Pallas kernels  103 us (99%)
  between operations  1.29 us (1%)
    pallas_call x1, Pallas kernels, shards(): pl.pallas_call(kernel, out_shape=shapes(BF), in_specs=[free, free, free,...  96.6 us
    pallas_call x1, Pallas kernels, shards(): pl.pallas_call(densify, out_shape=jax.ShapeDtypeStruct((n_col, rows, span...  4.01 us
    pallas_call x1, Pallas kernels, shards(): pl.pallas_call(finish, out_shape=shapes(F32), in_specs=[vmem] * 3, out_sp...  2.36 us

profile of v3, /device:TPU:0, one launch (start us, length us, event | category | flops | bytes accessed | tf_op | source)
XLA Modules:
  0.0 104.3 jit_solution(17555683588788418296)
XLA Ops:
  1.3 4.0 %shard_map.94.a = bf16[8,256,1024]{2,1,0:T(8,128)(2,1)} custom-call(bf16[32,128,128]{2,1,0:T(8,128)(2,1)} %bitcast.5, s32[32]{0:T(128)} %bitcast.6, s32[32]{0:T(128)} %bitcast.7, s32[1]{0:T(128)} %bitcast.4.count), custom_call_target="tpu_custom_call" | custom-call | tf_op jit(solution)/shard_map/pallas_call | solution.py:460
  5.3 96.6 %shard_map.95 = (bf16[256,512]{1,0:T(8,128)(2,1)}, bf16[256,512]{1,0:T(8,128)(2,1)}, bf16[512,512]{1,0:T(8,128)(2,1)}) custom-call(bf16[256,512]{1,0:T(8,128)(2,1)} %feat.1, bf16[512,512]{1,0:T(8,128)(2,1)} %w.1, bf16[8,256,1024]{2,1,0:T(8,128)(2,1)} %shard_map.94.a, bf16[256,512]{1,0:T(8,128)(2,1)} %cot.1), custom_call_target="tpu_custom_call" | custom-call | tf_op jit(solution)/shard_map/pallas_call | solution.py:535
  101.9 2.4 %shard_map.96 = (bf16[256,512]{1,0:T(8,128)(2,1)}, bf16[256,512]{1,0:T(8,128)(2,1)}, f32[512,512]{1,0:T(8,128)}) custom-call(bf16[256,512]{1,0:T(8,128)(2,1)} %get-tuple-element.6.out_in, bf16[256,512]{1,0:T(8,128)(2,1)} %get-tuple-element.7.gfeat_in, bf16[512,512]{1,0:T(8,128)(2,1)} %get-tuple-element.8.gweight_in), custom_call_target="tpu_custom_call" | custom-call | tf_op jit(solution)/shard_map/pallas_call | solution.py:546
